TPU v7x, 512 devices: a whole 4x8x8 slice. The times are simulated.
512 devices in a mesh: samp: 64 (over z_hi, y, x), par: 8 (over z_lo, core).
Axes of the slice: x: 4, y: 8, z: 8 (z_hi: 2, z_lo: 4; z = z_hi * 4 + z_lo), core: 2. Of those that a mesh axis runs over, the one named last changes fastest.
Arguments:
- hidden: bfloat16 [64, 256, 1024], P('samp'), may hold values from -6 to 6
- configs: int32 [64, 256], P('samp'), may hold values from 0 to 3
- embed: bfloat16 [4, 1024], replicated, may hold values from -6 to 6
- w_up: bfloat16 [1024, 4096], P(None, 'par'), may hold values from -0.1875 to 0.1875
- readout: float32 [4096], P('par'), may hold values from -6 to 6
- energies: float32 [64], P('samp'), may hold values from -12 to 12
Outputs:
- update: float32 [1024, 4096], P('samp', 'par')
All inputs are finite; a program needn't handle non-finite values.
Results may differ from a plain program's by a relative error of at most 0.02.
The roundings to bfloat16 on the way count: a program that leaves them out, or rounds other values in their place, can miss the bound.
Values may be sent and summed in bfloat16 or wider, within the bound.
A program may use at most 64 MiB of HBM per device.

v0:
```python
import math

import jax
import jax.numpy as jnp
from jax import lax
from jax.sharding import PartitionSpec as P

norm_eps = 1e-06
diag_shift = 0.1


def features(hidden, configs, embed):
    levels = embed.shape[0]
    onehot = (configs[:, :, None] == jnp.arange(levels, dtype=jnp.int32)).astype(jnp.bfloat16)
    added = jnp.einsum("sto,od->std", onehot, embed, preferred_element_type=jnp.float32)
    summed = hidden.astype(jnp.float32) + added
    scale = lax.rsqrt(jnp.mean(summed * summed, axis=-1, keepdims=True) + norm_eps)
    return (summed * scale).astype(jnp.bfloat16)


def slope_of(preact):
    sigma = jax.nn.sigmoid(preact)
    return sigma * (1.0 + preact * (1.0 - sigma))


def solve_weights(gram, energy_all):
    count = gram.shape[0]
    trace_mean = jnp.trace(gram) / count
    system = gram + diag_shift * trace_mean * jnp.eye(count, dtype=gram.dtype)
    factor = jnp.linalg.cholesky(system)
    centered_e = (energy_all - jnp.mean(energy_all)) / math.sqrt(count)
    weights = jax.scipy.linalg.cho_solve((factor, True), centered_e)
    return (weights.astype(jnp.bfloat16), trace_mean)


def shards(hidden, configs, embed, w_up, readout, energies):
    normed = features(hidden, configs, embed)
    preact = jnp.einsum("std,df->stf", normed, w_up, preferred_element_type=jnp.float32)
    signal = (readout * slope_of(preact)).astype(jnp.bfloat16)
    jacobian = jnp.einsum(
        "std,stf->sdf", normed, signal, preferred_element_type=jnp.float32
    ).astype(jnp.bfloat16)
    moved = lax.all_to_all(jacobian, "samp", split_axis=1, concat_axis=0, tiled=True)
    total = moved.shape[0]
    flat = moved.reshape(total, -1)
    mean_row = jnp.mean(flat, axis=0, dtype=jnp.float32)
    centered = ((flat.astype(jnp.float32) - mean_row) / math.sqrt(total)).astype(jnp.bfloat16)
    partial_gram = lax.dot_general(
        centered, centered, (((1,), (1,)), ((), ())), preferred_element_type=jnp.float32
    )
    energy_all = lax.all_gather(energies, "samp", axis=0, tiled=True)
    gram = lax.psum(partial_gram, ("samp", "par"))
    weights, trace_mean = solve_weights(gram, energy_all)
    applied = jnp.dot(weights[None, :], centered, preferred_element_type=jnp.float32)
    piece = -trace_mean * applied.reshape(moved.shape[1:])
    return piece


def solution(mesh):
    in_specs = (P("samp", None, None), P("samp", None), P(), P(None, "par"), P("par"), P("samp"))
    out_specs = P("samp", "par")
    return jax.shard_map(shards, mesh=mesh, in_specs=in_specs, out_specs=out_specs, check_vma=False)
```

profile of v0, /device:TPU:1, one launch (start us, length us, event | category | flops | bytes accessed | tf_op | source)
XLA Modules:
  0.0 401.7 jit_solution(17000444009299961397)
XLA Ops:
  0.0 0.0 copy-start
  0.0 1.6 multiply_reduce_fusion
  1.6 2.7 fusion.2
  4.3 2.8 copy.34
  7.1 0.5 broadcast.142
  7.6 8.1 %reduce.10 = bf16[1024,512]{1,0:T(8,128)(2,1)} reduce(bf16[1024,1,512]{2,1,0:T(2,128)(2,1)S(1)} %bitcast.73, bf16[]{:T(256)} %broadcast.142), dimensions={1}, to_apply=%bitcast.68.reduce_sub_computation | reduce | bytes 2097154
  15.7 2.6 reshape.152
  18.4 19.8 %all-to-all-start = ((bf16[64,2,4096]{2,1,0:T(2,128)(2,1)}), bf16[64,2,4096]{2,1,0:T(2,128)(2,1)}, u32[]{:S(2)}, u32[]{:S(2)}) async-start(bf16[64,2,4096]{2,1,0:T(2,128)(2,1)} %reshape.152), calls=%async_computation | async-start | bytes 2097152 | tf_op jit(solution)/shard_map/all_to_all | solution.py:43
  38.8 1.3 dynamic-slice
  40.1 0.8 dynamic-update-slice.3
  40.9 203.4 %all-reduce = f32[64]{0:T(128)S(1)} all-reduce(f32[64]{0:T(128)S(1)} %dynamic-update-slice.3), channel_id=1, replica_groups=mesh['samp'=64,'par'=8] {'samp'}, use_global_device_ids=true, to_apply=%add | all-reduce | flops 64 | bytes 512
  244.3 0.6 reduce_sum.40
  245.6 0.0 all-to-all-done
  245.6 6.5 %reshape.153 = bf16[1024,1,512]{2,1,0:T(2,128)(2,1)S(1)} reshape(bf16[64,2,4096]{2,1,0:T(2,128)(2,1)} %all-to-all-done) | data formatting | bytes 2097152
  252.1 1.6 copy_convert_fusion
  253.6 2.7 reshape.139
  256.4 1.7 reduce_sum.38
  258.1 0.2 sub.32
  258.4 0.6 fusion.1
  258.9 2.3 convolution_bitcast_fusion.1
  261.2 124.9 %psum.7 = f32[64,64]{1,0:T(8,128)S(1)} all-reduce(f32[64,64]{1,0:T(8,128)S(1)} %convolution_bitcast_fusion.1), channel_id=1, replica_groups=mesh['samp'=64,'par'=8] {'samp','par'}, use_global_device_ids=true, to_apply=%region_2.0 | all-reduce | flops 4096 | bytes 32768 | tf_op jit(solution)/shard_map/psum | solution.py:52
  386.1 0.6 select_reduce_fusion.1
  388.1 0.1 copy.18
  388.2 5.8 %cholesky.13 = f32[64,64]{1,0:T(8,128)S(1)} custom-call(f32[64,64]{1,0:T(8,128)S(1)} %fusion.17), custom_call_target="Cholesky" | custom-call | tf_op jit(solution)/shard_map/jit(cholesky)/cholesky | solution.py:30
  394.1 0.6 compare_reduce_fusion
  394.7 0.7 fusion.14
  395.4 4.9 %custom-call.10 = f32[1,64,64]{1,2,0:T(8,128)S(1)} custom-call(f32[1,64,64]{2,1,0:T(8,128)S(1)} %fusion.14), custom_call_target="InvertDiagBlocksLowerTriangular" | custom-call | tf_op jit(solution)/shard_map/jit(_cho_solve)/triangular_solve | solution.py:32
  400.3 0.2 convolution_bitcast_fusion.3
  400.4 0.2 fusion.5
  400.6 0.2 multiply_convert_fusion
  400.8 0.2 fusion.6
  401.1 0.6 bitcast_multiply_fusion
  (10 shorter events, 0.1 us)
Async XLA Ops:
  0.0 1.6 copy-start
  18.4 227.2 %all-to-all-start = ((bf16[64,2,4096]{2,1,0:T(2,128)(2,1)}), bf16[64,2,4096]{2,1,0:T(2,128)(2,1)}, u32[]{:S(2)}, u32[]{:S(2)}) async-start(bf16[64,2,4096]{2,1,0:T(2,128)(2,1)} %reshape.152), calls=%async_computation | async-start | bytes 2097152 | tf_op jit(solution)/shard_map/all_to_all | solution.py:43
  258.9 141.7 %copy-start.1 = (f32[64,8192]{1,0:T(8,128)S(1)}, f32[64,8192]{1,0:T(8,128)}, u32[]{:S(2)}) copy-start(f32[64,8192]{1,0:T(8,128)} %reshape.139) | copy-start | bytes 6291460
where the time goes:
time: 402 us
  blocking collectives  328 us (82%)
  other arithmetic  26.1 us (6%)
  starting transfers between devices  19.8 us (5%)
  local copies, waits for them, and re-layouts  17.6 us (4%)
  matrix products  7.08 us (2%)
    unnamed x1, blocking collectives  203 us
    psum x1, blocking collectives, shards(): gram = lax.psum(partial_gram, ('samp', 'par'))  125 us
    all_to_all x1, starting transfers between devices, shards(): lax.all_to_all(jacobian, 'samp', split_axis=1, concat_axis=0, tiled=True)  19.8 us
    unnamed x11, local copies, waits for them, and re-layouts  11.7 us
    unnamed x2, other arithmetic  8.08 us
  transfers between devices with their start and end apart: 1, of which 0 were waited for; matrix products, arithmetic and copies ran while one was open for 1% of the time, Pallas kernels for 0%

commit v1 on v0

v1 whole, which is shorter than its diff:
```python
import functools

import jax
import jax.numpy as jnp
from jax import lax
from jax.experimental import pallas as pl
from jax.experimental.pallas import tpu as pltpu
from jax.sharding import PartitionSpec as P

norm_eps = 1e-06
diag_shift = 0.1
MESH = pl.DeviceIdType.MESH
COUNT = 64
ROWS = 16
NT = (((1,), (1,)), ((), ()))


def place():
    s = lax.axis_index("samp")
    p = lax.axis_index("par")
    return s // 32, (s // 4) % 8, s % 4, p // 2, p % 2


def samp_of(zh, y, x):
    return (zh * 8 + y) * 4 + x


def slope_of(z):
    sigma = 1.0 / (1.0 + jnp.exp(-z))
    return sigma * (1.0 + z * (1.0 - sigma))


def kernel(
    hidden, configs, embed, w_up, readout, energy, out,
    normed_t, jac, recv, cent, flat, part, buf_a, buf_b, buf_c, buf_d, scale,
    send_sem, recv_sem, ar_send, ar_recv,
):
    zh, y, x, zl, c = place()
    me = samp_of(zh, y, x)
    mypar = zl * 2 + c
    z = zh * 4 + zl
    slot_a = x * 2 + c

    barrier = pltpu.get_barrier_semaphore()

    def greet(d, carry):
        t = lax.rem(me + d, COUNT)
        pl.semaphore_signal(barrier, inc=1, device_id=(t, mypar), device_id_type=MESH)
        return carry

    lax.fori_loop(1, COUNT, greet, 0)
    for dx in range(4):
        pl.semaphore_signal(
            barrier, inc=1,
            device_id=(samp_of(zh, y, (x + dx) % 4), zl * 2 + (1 - c)), device_id_type=MESH)
    for dz in (1, 2, 3, 5, 6, 7):
        zt = (z + dz) % 8
        pl.semaphore_signal(
            barrier, inc=1,
            device_id=(samp_of(zt // 4, y, x), (zt % 4) * 2 + c), device_id_type=MESH)

    cfg = jnp.broadcast_to(configs[...].astype(jnp.float32), (8, 256)).T[:, 0:1]
    added = jnp.zeros((256, 1024), jnp.float32)
    for level in range(4):
        row = embed[level:level + 1, :].astype(jnp.float32)
        added = jnp.where(cfg == float(level), row, added)
    summed = hidden[0].astype(jnp.float32) + added
    norm = lax.rsqrt(jnp.mean(summed * summed, axis=-1, keepdims=True) + norm_eps)
    wide = summed * norm
    normed = wide.astype(jnp.bfloat16)
    normed_t[...] = normed.T
    preact = jnp.dot(normed, w_up[...], preferred_element_type=jnp.float32)
    signal = (readout[...] * slope_of(preact)).astype(jnp.bfloat16)

    def piece(dz, dq):
        yq = (y // 2 + dq) % 4
        zt = (zh + dz) % 2
        base = pl.multiple_of(samp_of(zt, yq * 2, 0) * ROWS, 128)
        block = jnp.dot(normed_t[pl.ds(base, 128), :], signal, preferred_element_type=jnp.float32)
        jac[pl.ds(base, 128), :] = block.astype(jnp.bfloat16)
        return zt, yq

    def send(zt, yq, dr, dx):
        t = samp_of(zt, yq * 2 + (y + dr) % 2, (x + dx) % 4)
        pltpu.make_async_remote_copy(
            src_ref=jac.at[pl.ds(pl.multiple_of(t * ROWS, ROWS), ROWS)],
            dst_ref=recv.at[me],
            send_sem=send_sem,
            recv_sem=recv_sem,
            device_id=(t, mypar),
            device_id_type=MESH,
        ).start()

    order = [(dr, dx) for dx in (0, 1, 3, 2) for dr in (0, 1)]
    zt, yq = piece(0, 0)
    pl.semaphore_wait(barrier, 73)
    for dr, dx in order[1:]:
        send(zt, yq, dr, dx)
    recv[me] = jac[pl.ds(pl.multiple_of(me * ROWS, ROWS), ROWS), :]

    def later(n, carry):
        zt, yq = piece(n % 2, n // 2)
        for dr, dx in order:
            send(zt, yq, dr, dx)
        return carry

    lax.fori_loop(1, 8, later, 0)

    pltpu.make_async_copy(recv.at[pl.ds(0, 63)], recv.at[pl.ds(0, 63)], recv_sem).wait()

    def add(s, total):
        return total + recv[s].astype(jnp.float32)

    total = lax.fori_loop(0, COUNT, add, jnp.zeros((ROWS, 512), jnp.float32), unroll=8)
    mean = total * (1.0 / COUNT)

    def center(s, carry):
        v = ((recv[s].astype(jnp.float32) - mean) * 0.125).astype(jnp.bfloat16)
        for j in range(4):
            cent[j, pl.ds(pl.multiple_of(s * ROWS, ROWS), ROWS), :] = (
                v[:, j * 128:(j + 1) * 128].astype(jnp.float32))
        return carry

    lax.fori_loop(0, COUNT, center, 0, unroll=8)

    for i in range(ROWS):
        for j in range(4):
            at = (i * 4 + j) * 128
            flat[:, at:at + 128] = cent[j, pl.ds(i, COUNT, stride=ROWS), :].astype(jnp.bfloat16)
    gram = lax.dot_general(flat[...], flat[...], NT, preferred_element_type=jnp.float32)
    rows = lax.broadcasted_iota(jnp.int32, (COUNT, COUNT), 0)
    lanes = lax.broadcasted_iota(jnp.int32, (COUNT, COUNT), 1)
    side = jnp.where((rows == me) & (lanes == 0), energy[0] * 0.125, 0.0)
    part[...] = jnp.concatenate([gram, side], axis=1).reshape(8, 8, 128)

    def exchange(buf, n, slot, src_of, target_of, own):
        copies = []
        for d in range(1, n):
            copy = pltpu.make_async_remote_copy(
                src_ref=src_of(d), dst_ref=buf.at[slot],
                send_sem=ar_send.at[own], recv_sem=ar_recv.at[own],
                device_id=target_of(d), device_id_type=MESH)
            copy.start()
        return copies

    def settle(buf, own):
        pltpu.make_async_copy(buf.at[pl.ds(0, 7)], buf.at[pl.ds(0, 7)], ar_recv.at[own]).wait()

    def settle_send(buf, own):
        pltpu.make_async_copy(buf.at[pl.ds(0, 7)], buf.at[pl.ds(0, 7)], ar_send.at[own]).wait()

    def peer_a(d):
        xt = (x + d // 2) % 4
        ct = (c + d) % 2
        return xt, ct

    def src_a(d):
        xt, ct = peer_a(d)
        return part.at[xt * 2 + ct]

    def dev_a(d):
        xt, ct = peer_a(d)
        return (samp_of(zh, y, xt), zl * 2 + ct)

    def dev_b(d):
        return (samp_of(zh, (y + d) % 8, x), mypar)

    def dev_c(d):
        zt = (z + d) % 8
        return (samp_of(zt // 4, y, x), (zt % 4) * 2 + c)

    exchange(buf_a, 8, slot_a, src_a, dev_a, 0)
    buf_a[slot_a] = part[slot_a]
    settle(buf_a, 0)
    buf_b[y] = jnp.sum(buf_a[...], axis=0)
    exchange(buf_b, 8, y, lambda d: buf_b.at[y], dev_b, 1)
    settle(buf_b, 1)
    buf_c[z] = jnp.sum(buf_b[...], axis=0)
    exchange(buf_c, 8, z, lambda d: buf_c.at[z], dev_c, 2)
    settle(buf_c, 2)
    buf_d[slot_a] = jnp.sum(buf_c[...], axis=0)
    exchange(buf_d, 8, slot_a, lambda d: buf_d.at[slot_a], dev_a, 3)
    settle(buf_d, 3)

    full = buf_d[...].reshape(COUNT, 128)
    row = lax.broadcasted_iota(jnp.int32, (COUNT, 128), 0)
    lane = lax.broadcasted_iota(jnp.int32, (COUNT, 128), 1)
    diag = row == lane
    trace_mean = jnp.sum(jnp.where(diag, full, 0.0), keepdims=True) * (1.0 / COUNT)
    right = lane == COUNT
    mean_e = jnp.sum(jnp.where(right, full, 0.0), keepdims=True) * (1.0 / COUNT)
    m = jnp.where(right, (full - mean_e) * 0.125, full + jnp.where(diag, diag_shift * trace_mean, 0.0))
    for k in range(COUNT):
        pivot = m[k:k + 1, :] * (1.0 / m[k:k + 1, k:k + 1])
        m = jnp.where(row == k, pivot, m - m[:, k:k + 1] * pivot)
    weights = m[:, COUNT:COUNT + 1].astype(jnp.bfloat16).astype(jnp.float32)
    scale[...] = jnp.broadcast_to(weights, (COUNT, 128))

    def apply(s, acc):
        w = scale[pl.ds(s, 1), :]
        at = pl.ds(pl.multiple_of(s * ROWS, ROWS), ROWS)
        return tuple(a + w * cent[j, at, :] for j, a in enumerate(acc))

    zero = jnp.zeros((ROWS, 128), jnp.float32)
    applied = lax.fori_loop(0, COUNT, apply, (zero,) * 4, unroll=8)
    for j in range(4):
        out[:, j * 128:(j + 1) * 128] = -trace_mean * applied[j]

    pltpu.make_async_copy(recv.at[pl.ds(0, 63)], recv.at[pl.ds(0, 63)], send_sem).wait()
    for own, buf in enumerate((buf_a, buf_b, buf_c, buf_d)):
        settle_send(buf, own)


def shards(hidden, configs, embed, w_up, readout, energies):
    vmem = pl.BlockSpec(memory_space=pltpu.VMEM)
    smem = pl.BlockSpec(memory_space=pltpu.SMEM)
    tile = pltpu.VMEM((8, 8, 128), jnp.float32)
    return pl.pallas_call(
        kernel,
        out_shape=jax.ShapeDtypeStruct((ROWS, 512), jnp.float32),
        in_specs=[vmem, vmem, vmem, vmem, vmem, smem],
        out_specs=vmem,
        scratch_shapes=[
            pltpu.VMEM((1024, 256), jnp.bfloat16),
            pltpu.VMEM((1024, 512), jnp.bfloat16),
            pltpu.VMEM((COUNT, ROWS, 512), jnp.bfloat16),
            pltpu.VMEM((4, COUNT * ROWS, 128), jnp.float32),
            pltpu.VMEM((COUNT, 8192), jnp.bfloat16),
            tile, tile, tile, tile, tile,
            pltpu.VMEM((COUNT, 128), jnp.float32),
            pltpu.SemaphoreType.DMA,
            pltpu.SemaphoreType.DMA,
            pltpu.SemaphoreType.DMA((4,)),
            pltpu.SemaphoreType.DMA((4,)),
        ],
        compiler_params=pltpu.CompilerParams(
            collective_id=0, has_side_effects=True, vmem_limit_bytes=48 << 20),
        name="step",
    )(hidden, configs, embed, w_up, readout.reshape(1, 512), energies)


def solution(mesh):
    in_specs = (P("samp", None, None), P("samp", None), P(), P(None, "par"), P("par"), P("samp"))
    out_specs = P("samp", "par")
    return jax.shard_map(shards, mesh=mesh, in_specs=in_specs, out_specs=out_specs, check_vma=False)
```

time: 402 us -> 78 us (0.19)
  blocking collectives: 328 us -> 0 us
  Pallas kernels: 0 us -> 72.8 us
  other arithmetic: 26.1 us -> 0 us
  starting transfers between devices: 19.8 us -> 0 us
  local copies, waits for them, and re-layouts: 17.6 us -> 4.25 us
  matrix products: 7.08 us -> 0 us
    unnamed x1 -> x0, blocking collectives: 203 us -> none
    psum x1 -> x0, blocking collectives: 125 us -> none  [shards(): gram = lax.psum(partial_gram, ('samp', 'par'))]
    pallas_call x0 -> x1, Pallas kernels: none -> 72.8 us  [shards(): pl.pallas_call(kernel, out_shape=jax.ShapeDtypeStruct((ROWS, 512), jnp.fl...]
    all_to_all x1 -> x0, starting transfers between devices: 19.8 us -> none  [shards(): lax.all_to_all(jacobian, 'samp', split_axis=1, concat_axis=0, tiled=True)]
    another operation x5 -> x0, other arithmetic: 12.1 us -> none  [the longest x3 6.52 us: solve_weights(): factor = jnp.linalg.cholesky(system)]
    unnamed x2 -> x0, other arithmetic: 8.08 us -> none
    unnamed x11, local copies, waits for them, and re-layouts: 11.7 us -> 4.25 us
    dot_general x4 -> x0, matrix products: 6.77 us -> none  [the longest x1 2.68 us: shards(): jnp.einsum('std,stf->sdf', normed, signal, preferred_element_type=jnp.flo...]
  transfers between devices with their start and end apart: 1 -> 0, of which waited for: 0 -> 0; matrix products, arithmetic and copies ran while one was open for 1% -> 0% of each run, Pallas kernels for 0% -> 0%
where the time goes in v1:
time: 78 us; the launch traced here: 77.7 us
  Pallas kernels  72.8 us (93%)
  local copies, waits for them, and re-layouts  4.25 us (5%)
    pallas_call x1, Pallas kernels, shards(): pl.pallas_call(kernel, out_shape=jax.ShapeDtypeStruct((ROWS, 512), jnp.fl...  72.8 us
    unnamed x11, local copies, waits for them, and re-layouts  4.25 us

profile of v1, /device:TPU:1, one launch (start us, length us, event | category | flops | bytes accessed | tf_op | source)
XLA Modules:
  0.0 77.7 jit_solution(1828015346810312955)
XLA Ops:
  0.0 0.0 copy-start.3
  0.7 0.0 copy-start.4
  0.7 0.0 copy-done.3
  0.7 0.7 copy-done.4
  1.3 0.0 copy-start
  1.4 1.2 %copy-done = bf16[1024,512]{1,0:T(8,128)(2,1)S(1)} copy-done((bf16[1024,512]{1,0:T(8,128)(2,1)S(1)}, bf16[1024,512]{1,0:T(8,128)(2,1)}, u32[]{:S(2)}) %copy-start) | copy-done | bytes 1048600
  2.6 0.0 copy-start.1
  2.6 1.0 %copy-done.1 = bf16[1,256,1024]{2,1,0:T(8,128)(2,1)S(1)} copy-done((bf16[1,256,1024]{2,1,0:T(8,128)(2,1)S(1)}, bf16[1,256,1024]{2,1,0:T(8,128)(2,1)}, u32[]{:S(2)}) %copy-start.1) | copy-done | bytes 524312
  3.6 0.0 copy-start.2
  3.6 0.7 copy-done.2
  4.3 72.8 %step.1 = f32[16,512]{1,0:T(8,128)S(1)} custom-call(bf16[1,256,1024]{2,1,0:T(8,128)(2,1)S(1)} %copy-done.1, s32[1,256]{1,0:T(1,128)S(1)} %copy-done.4, bf16[4,1024]{1,0:T(4,128)(2,1)S(1)} %copy-done.2, bf16[1024,512]{1,0:T(8,128)(2,1)S(1)} %copy-done, f32[1,512]{1,0:T(1,128)S(1)} %bitcast.1, f32[1]{0:T(128)S(6)} %copy.8.energy), custom_call_target="tpu_custom_call" | custom-call | tf_op jit(solution)/shard_map/step/pallas_call | solution.py:218
  77.1 0.6 copy.9
Async XLA Ops:
  0.0 0.7 copy-start.3
  0.7 0.7 copy-start.4
  1.3 1.2 %copy-start = (bf16[1024,512]{1,0:T(8,128)(2,1)S(1)}, bf16[1024,512]{1,0:T(8,128)(2,1)}, u32[]{:S(2)}) copy-start(bf16[1024,512]{1,0:T(8,128)(2,1)} %w_up.1) | copy-start | bytes 3145732
  2.6 1.0 %copy-start.1 = (bf16[1,256,1024]{2,1,0:T(8,128)(2,1)S(1)}, bf16[1,256,1024]{2,1,0:T(8,128)(2,1)}, u32[]{:S(2)}) copy-start(bf16[1,256,1024]{2,1,0:T(8,128)(2,1)} %hidden.1) | copy-start | bytes 1572868
  3.6 0.7 copy-start.2

commit v2 on v1

--- a/solution.py
+++ b/solution.py
@@ -12,6 +12,8 @@
 MESH = pl.DeviceIdType.MESH
 COUNT = 64
 ROWS = 16
+HALF = 32
+PANEL = 8
 NT = (((1,), (1,)), ((), ()))
 
 
@@ -31,9 +33,10 @@
 
 
 def kernel(
-    hidden, configs, embed, w_up, readout, energy, out,
-    normed_t, jac, recv, cent, flat, part, buf_a, buf_b, buf_c, buf_d, scale,
-    send_sem, recv_sem, ar_send, ar_recv,
+    hidden_in, configs_in, embed_in, w_in, readout_in, energy_in, out,
+    hidden, configs, embed, w_up, readout, energy,
+    normed_t, jac, recv, cent, flat, buf_a, buf_b, buf_c, scale,
+    in_sem, send_sem, recv_sem, ar_send, ar_recv,
 ):
     zh, y, x, zl, c = place()
     me = samp_of(zh, y, x)
@@ -59,16 +62,29 @@
             barrier, inc=1,
             device_id=(samp_of(zt // 4, y, x), (zt % 4) * 2 + c), device_id_type=MESH)
 
+    loads = [
+        pltpu.make_async_copy(src, dst, in_sem.at[n])
+        for n, (src, dst) in enumerate((
+            (configs_in, configs), (embed_in, embed), (hidden_in, hidden),
+            (readout_in, readout), (w_in, w_up), (energy_in, energy)))
+    ]
+    for load in loads:
+        load.start()
+    for load in loads[:3]:
+        load.wait()
+
     cfg = jnp.broadcast_to(configs[...].astype(jnp.float32), (8, 256)).T[:, 0:1]
     added = jnp.zeros((256, 1024), jnp.float32)
     for level in range(4):
         row = embed[level:level + 1, :].astype(jnp.float32)
         added = jnp.where(cfg == float(level), row, added)
-    summed = hidden[0].astype(jnp.float32) + added
+    summed = hidden[...].astype(jnp.float32) + added
     norm = lax.rsqrt(jnp.mean(summed * summed, axis=-1, keepdims=True) + norm_eps)
     wide = summed * norm
     normed = wide.astype(jnp.bfloat16)
     normed_t[...] = normed.T
+    for load in loads[3:]:
+        load.wait()
     preact = jnp.dot(normed, w_up[...], preferred_element_type=jnp.float32)
     signal = (readout[...] * slope_of(preact)).astype(jnp.bfloat16)
 
@@ -128,39 +144,31 @@
             at = (i * 4 + j) * 128
             flat[:, at:at + 128] = cent[j, pl.ds(i, COUNT, stride=ROWS), :].astype(jnp.bfloat16)
     gram = lax.dot_general(flat[...], flat[...], NT, preferred_element_type=jnp.float32)
-    rows = lax.broadcasted_iota(jnp.int32, (COUNT, COUNT), 0)
-    lanes = lax.broadcasted_iota(jnp.int32, (COUNT, COUNT), 1)
-    side = jnp.where((rows == me) & (lanes == 0), energy[0] * 0.125, 0.0)
-    part[...] = jnp.concatenate([gram, side], axis=1).reshape(8, 8, 128)
-
-    def exchange(buf, n, slot, src_of, target_of, own):
-        copies = []
-        for d in range(1, n):
-            copy = pltpu.make_async_remote_copy(
-                src_ref=src_of(d), dst_ref=buf.at[slot],
+    up, left, low = gram[:HALF, :HALF], gram[HALF:, :HALF], gram[HALF:, HALF:]
+    r32 = lax.broadcasted_iota(jnp.int32, (HALF, HALF), 0)
+    c32 = lax.broadcasted_iota(jnp.int32, (HALF, HALF), 1)
+    both = jnp.concatenate([jnp.where(c32 <= r32, up, low), left], axis=1)
+    low_diag = jnp.sum(jnp.where(c32 == r32, low, 0.0), axis=0, keepdims=True)
+    low_diag = jnp.concatenate([low_diag, jnp.zeros((1, 128 - HALF), jnp.float32)], axis=1)
+    tail_row = lax.broadcasted_iota(jnp.int32, (8, 128), 0)
+    tail_lane = lax.broadcasted_iota(jnp.int32, (8, 128), 1)
+    mine = jnp.where((tail_row == 1) & (tail_lane == me), energy[...] * 0.125, 0.0)
+    buf_a[slot_a, 0:16] = jnp.concatenate([both[:16], both[16:]], axis=1)
+    buf_a[slot_a, 16:24] = jnp.where(tail_row == 0, low_diag, mine)
+
+    def exchange(buf, slot, target_of, own):
+        for d in range(1, 8):
+            pltpu.make_async_remote_copy(
+                src_ref=buf.at[slot], dst_ref=buf.at[slot],
                 send_sem=ar_send.at[own], recv_sem=ar_recv.at[own],
-                device_id=target_of(d), device_id_type=MESH)
-            copy.start()
-        return copies
-
-    def settle(buf, own):
+                device_id=target_of(d), device_id_type=MESH).start()
         pltpu.make_async_copy(buf.at[pl.ds(0, 7)], buf.at[pl.ds(0, 7)], ar_recv.at[own]).wait()
 
     def settle_send(buf, own):
         pltpu.make_async_copy(buf.at[pl.ds(0, 7)], buf.at[pl.ds(0, 7)], ar_send.at[own]).wait()
 
-    def peer_a(d):
-        xt = (x + d // 2) % 4
-        ct = (c + d) % 2
-        return xt, ct
-
-    def src_a(d):
-        xt, ct = peer_a(d)
-        return part.at[xt * 2 + ct]
-
     def dev_a(d):
-        xt, ct = peer_a(d)
-        return (samp_of(zh, y, xt), zl * 2 + ct)
+        return (samp_of(zh, y, (x + d // 2) % 4), zl * 2 + (c + d) % 2)
 
     def dev_b(d):
         return (samp_of(zh, (y + d) % 8, x), mypar)
@@ -169,30 +177,41 @@
         zt = (z + d) % 8
         return (samp_of(zt // 4, y, x), (zt % 4) * 2 + c)
 
-    exchange(buf_a, 8, slot_a, src_a, dev_a, 0)
-    buf_a[slot_a] = part[slot_a]
-    settle(buf_a, 0)
+    exchange(buf_a, slot_a, dev_a, 0)
     buf_b[y] = jnp.sum(buf_a[...], axis=0)
-    exchange(buf_b, 8, y, lambda d: buf_b.at[y], dev_b, 1)
-    settle(buf_b, 1)
+    exchange(buf_b, y, dev_b, 1)
     buf_c[z] = jnp.sum(buf_b[...], axis=0)
-    exchange(buf_c, 8, z, lambda d: buf_c.at[z], dev_c, 2)
-    settle(buf_c, 2)
-    buf_d[slot_a] = jnp.sum(buf_c[...], axis=0)
-    exchange(buf_d, 8, slot_a, lambda d: buf_d.at[slot_a], dev_a, 3)
-    settle(buf_d, 3)
-
-    full = buf_d[...].reshape(COUNT, 128)
+    exchange(buf_c, z, dev_c, 2)
+    whole = jnp.sum(buf_c[...], axis=0)
+
+    both = jnp.concatenate([whole[:16, :COUNT], whole[:16, COUNT:]], axis=0)
+    turned = jnp.concatenate([both, jnp.zeros((HALF, COUNT), jnp.float32)], axis=1).T
+    mixed, mixed_t = both[:, :HALF], turned[:HALF]
+    up = jnp.where(c32 <= r32, mixed, mixed_t)
+    low = jnp.where(c32 > r32, mixed, jnp.where(c32 == r32, whole[16:17, :HALF], mixed_t))
+    spare = jnp.zeros((HALF, COUNT), jnp.float32)
+    full = jnp.concatenate([
+        jnp.concatenate([up, turned[HALF:COUNT], spare], axis=1),
+        jnp.concatenate([both[:, HALF:], low, spare], axis=1)], axis=0)
+    energies = whole[17:18, :]
     row = lax.broadcasted_iota(jnp.int32, (COUNT, 128), 0)
     lane = lax.broadcasted_iota(jnp.int32, (COUNT, 128), 1)
     diag = row == lane
     trace_mean = jnp.sum(jnp.where(diag, full, 0.0), keepdims=True) * (1.0 / COUNT)
-    right = lane == COUNT
-    mean_e = jnp.sum(jnp.where(right, full, 0.0), keepdims=True) * (1.0 / COUNT)
-    m = jnp.where(right, (full - mean_e) * 0.125, full + jnp.where(diag, diag_shift * trace_mean, 0.0))
-    for k in range(COUNT):
-        pivot = m[k:k + 1, :] * (1.0 / m[k:k + 1, k:k + 1])
-        m = jnp.where(row == k, pivot, m - m[:, k:k + 1] * pivot)
+    mean_e = jnp.sum(energies, keepdims=True) * (1.0 / COUNT)
+    rhs = jnp.sum(jnp.where(diag, (energies - mean_e) * 0.125, 0.0), axis=1, keepdims=True)
+    m = jnp.where(lane == COUNT, rhs, full + jnp.where(diag, diag_shift * trace_mean, 0.0))
+    for first in range(0, COUNT, PANEL):
+        cols = [jnp.broadcast_to(m[:, k:k + 1], (COUNT, 128)) for k in range(first, first + PANEL)]
+        for j in range(PANEL):
+            k = first + j
+            col = cols[j]
+            inverse = 1.0 / col[k:k + 1, :]
+            pivot = m[k:k + 1, :] * inverse
+            m = jnp.where(row == k, pivot, m - col * pivot)
+            for n in range(j + 1, PANEL):
+                pivot = cols[n][k:k + 1, :] * inverse
+                cols[n] = jnp.where(row == k, pivot, cols[n] - col * pivot)
     weights = m[:, COUNT:COUNT + 1].astype(jnp.bfloat16).astype(jnp.float32)
     scale[...] = jnp.broadcast_to(weights, (COUNT, 128))
 
@@ -207,36 +226,39 @@
         out[:, j * 128:(j + 1) * 128] = -trace_mean * applied[j]
 
     pltpu.make_async_copy(recv.at[pl.ds(0, 63)], recv.at[pl.ds(0, 63)], send_sem).wait()
-    for own, buf in enumerate((buf_a, buf_b, buf_c, buf_d)):
+    for own, buf in enumerate((buf_a, buf_b, buf_c)):
         settle_send(buf, own)
 
 
 def shards(hidden, configs, embed, w_up, readout, energies):
+    hbm = pl.BlockSpec(memory_space=pltpu.HBM)
     vmem = pl.BlockSpec(memory_space=pltpu.VMEM)
-    smem = pl.BlockSpec(memory_space=pltpu.SMEM)
-    tile = pltpu.VMEM((8, 8, 128), jnp.float32)
+    args = (hidden[0], configs, embed, w_up, readout.reshape(1, 512), energies.reshape(1, 1))
+    held = [pltpu.VMEM(a.shape, a.dtype) for a in args]
+    sums = pltpu.VMEM((8, 24, 128), jnp.float32)
     return pl.pallas_call(
         kernel,
         out_shape=jax.ShapeDtypeStruct((ROWS, 512), jnp.float32),
-        in_specs=[vmem, vmem, vmem, vmem, vmem, smem],
+        in_specs=[hbm] * 6,
         out_specs=vmem,
-        scratch_shapes=[
+        scratch_shapes=held + [
             pltpu.VMEM((1024, 256), jnp.bfloat16),
             pltpu.VMEM((1024, 512), jnp.bfloat16),
             pltpu.VMEM((COUNT, ROWS, 512), jnp.bfloat16),
             pltpu.VMEM((4, COUNT * ROWS, 128), jnp.float32),
             pltpu.VMEM((COUNT, 8192), jnp.bfloat16),
-            tile, tile, tile, tile, tile,
+            sums, sums, sums,
             pltpu.VMEM((COUNT, 128), jnp.float32),
+            pltpu.SemaphoreType.DMA((6,)),
             pltpu.SemaphoreType.DMA,
             pltpu.SemaphoreType.DMA,
-            pltpu.SemaphoreType.DMA((4,)),
-            pltpu.SemaphoreType.DMA((4,)),
+            pltpu.SemaphoreType.DMA((3,)),
+            pltpu.SemaphoreType.DMA((3,)),
         ],
         compiler_params=pltpu.CompilerParams(
-            collective_id=0, has_side_effects=True, vmem_limit_bytes=48 << 20),
+            collective_id=0, has_side_effects=True, vmem_limit_bytes=56 << 20),
         name="step",
-    )(hidden, configs, embed, w_up, readout.reshape(1, 512), energies)
+    )(*args)
 
 
 def solution(mesh):

time: 78 us -> 69.6 us (0.89); the launches traced: 77.7 us -> 68.5 us
  Pallas kernels: 72.8 us -> 66.5 us
  local copies, waits for them, and re-layouts: 4.25 us -> 1.38 us
    pallas_call x1, Pallas kernels: 72.8 us -> 66.5 us  [shards(): pl.pallas_call(kernel, out_shape=jax.ShapeDtypeStruct((ROWS, 512), jnp.fl...]
    unnamed x11 -> x1, local copies, waits for them, and re-layouts: 4.25 us -> 1.38 us
where the time goes in v2:
time: 69.6 us; the launch traced here: 68.5 us
  Pallas kernels  66.5 us (96%)
  local copies, waits for them, and re-layouts  1.38 us (2%)
    pallas_call x1, Pallas kernels, shards(): pl.pallas_call(kernel, out_shape=jax.ShapeDtypeStruct((ROWS, 512), jnp.fl...  66.5 us

profile of v2, /device:TPU:1, one launch (start us, length us, event | category | flops | bytes accessed | tf_op | source)
XLA Modules:
  0.0 68.5 jit_solution(2109096085573453163)
XLA Ops:
  0.7 66.5 %step.1 = f32[16,512]{1,0:T(8,128)} custom-call(bf16[256,1024]{1,0:T(8,128)(2,1)} %bitcast.4, s32[1,256]{1,0:T(1,128)} %configs_in.1, bf16[4,1024]{1,0:T(4,128)(2,1)} %embed_in.1, bf16[1024,512]{1,0:T(8,128)(2,1)} %w_in.1, f32[1,512]{1,0:T(1,128)} %bitcast.5, f32[1,1]{1,0:T(1,128)} %bitcast.3.energy_in), custom_call_target="tpu_custom_call" | custom-call | tf_op jit(solution)/shard_map/step/pallas_call | solution.py:239
  67.1 1.4 %copy.9 = f32[16,512]{1,0:T(8,128)} copy(f32[16,512]{1,0:T(8,128)} %step.1) | data formatting | bytes 65536

commit v3 on v2

--- a/solution.py
+++ b/solution.py
@@ -14,6 +14,7 @@
 ROWS = 16
 HALF = 32
 PANEL = 8
+FAR = (4, 3, 5, 2, 6, 1, 7)
 NT = (((1,), (1,)), ((), ()))
 
 
@@ -46,21 +47,28 @@
 
     barrier = pltpu.get_barrier_semaphore()
 
-    def greet(d, carry):
-        t = lax.rem(me + d, COUNT)
-        pl.semaphore_signal(barrier, inc=1, device_id=(t, mypar), device_id_type=MESH)
-        return carry
-
-    lax.fori_loop(1, COUNT, greet, 0)
-    for dx in range(4):
+    for dz in FAR:
+        zt = (z + dz) % 8
+        if dz == 4:
+            continue
+        pl.semaphore_signal(
+            barrier, inc=1,
+            device_id=(samp_of(zt // 4, y, x), (zt % 4) * 2 + c), device_id_type=MESH)
+
+    ys = [(y + dy) % 8 for dy in FAR + (0,)]
+    xs = [(x + dx) % 4 for dx in (2, 1, 3, 0)]
+    for n, yt in enumerate(ys):
+        for zt in (1 - zh, zh):
+            line = (zt * 8 + yt) * 4
+            for k, xt in enumerate(xs):
+                if n == 7 and k == 3 and zt is zh:
+                    continue
+                pl.semaphore_signal(
+                    barrier, inc=1, device_id=(line + xt, mypar), device_id_type=MESH)
+    for dx in (2, 1, 3, 0):
         pl.semaphore_signal(
             barrier, inc=1,
             device_id=(samp_of(zh, y, (x + dx) % 4), zl * 2 + (1 - c)), device_id_type=MESH)
-    for dz in (1, 2, 3, 5, 6, 7):
-        zt = (z + dz) % 8
-        pl.semaphore_signal(
-            barrier, inc=1,
-            device_id=(samp_of(zt // 4, y, x), (zt % 4) * 2 + c), device_id_type=MESH)
 
     loads = [
         pltpu.make_async_copy(src, dst, in_sem.at[n])
@@ -96,8 +104,8 @@
         jac[pl.ds(base, 128), :] = block.astype(jnp.bfloat16)
         return zt, yq
 
-    def send(zt, yq, dr, dx):
-        t = samp_of(zt, yq * 2 + (y + dr) % 2, (x + dx) % 4)
+    def send(zt, yt, k):
+        t = (zt * 8 + yt) * 4 + xs[k]
         pltpu.make_async_remote_copy(
             src_ref=jac.at[pl.ds(pl.multiple_of(t * ROWS, ROWS), ROWS)],
             dst_ref=recv.at[me],
@@ -107,20 +115,16 @@
             device_id_type=MESH,
         ).start()
 
-    order = [(dr, dx) for dx in (0, 1, 3, 2) for dr in (0, 1)]
-    zt, yq = piece(0, 0)
-    pl.semaphore_wait(barrier, 73)
-    for dr, dx in order[1:]:
-        send(zt, yq, dr, dx)
+    sides = (y % 2, (y + 1) % 2)
+    for n, (dz, dq) in enumerate(((1, 2), (0, 2), (1, 1), (0, 1), (1, 3), (0, 3), (1, 0), (0, 0))):
+        zt, yq = piece(dz, dq)
+        if n == 0:
+            pl.semaphore_wait(barrier, 73)
+        for k in range(4):
+            for dr in (1, 0):
+                if (dz, dq, k, dr) != (0, 0, 3, 0):
+                    send(zt, yq * 2 + sides[dr], k)
     recv[me] = jac[pl.ds(pl.multiple_of(me * ROWS, ROWS), ROWS), :]
-
-    def later(n, carry):
-        zt, yq = piece(n % 2, n // 2)
-        for dr, dx in order:
-            send(zt, yq, dr, dx)
-        return carry
-
-    lax.fori_loop(1, 8, later, 0)
 
     pltpu.make_async_copy(recv.at[pl.ds(0, 63)], recv.at[pl.ds(0, 63)], recv_sem).wait()
 
@@ -154,10 +158,10 @@
     tail_lane = lax.broadcasted_iota(jnp.int32, (8, 128), 1)
     mine = jnp.where((tail_row == 1) & (tail_lane == me), energy[...] * 0.125, 0.0)
     buf_a[slot_a, 0:16] = jnp.concatenate([both[:16], both[16:]], axis=1)
-    buf_a[slot_a, 16:24] = jnp.where(tail_row == 0, low_diag, mine)
-
-    def exchange(buf, slot, target_of, own):
-        for d in range(1, 8):
+    buf_a[slot_a, 16:18] = jnp.where(tail_row == 0, low_diag, mine)[:2]
+
+    def exchange(buf, slot, target_of, own, steps):
+        for d in steps:
             pltpu.make_async_remote_copy(
                 src_ref=buf.at[slot], dst_ref=buf.at[slot],
                 send_sem=ar_send.at[own], recv_sem=ar_recv.at[own],
@@ -177,11 +181,11 @@
         zt = (z + d) % 8
         return (samp_of(zt // 4, y, x), (zt % 4) * 2 + c)
 
-    exchange(buf_a, slot_a, dev_a, 0)
+    exchange(buf_a, slot_a, dev_a, 0, (1, 2, 3, 4, 5, 6, 7))
     buf_b[y] = jnp.sum(buf_a[...], axis=0)
-    exchange(buf_b, y, dev_b, 1)
+    exchange(buf_b, y, dev_b, 1, range(1, 8))
     buf_c[z] = jnp.sum(buf_b[...], axis=0)
-    exchange(buf_c, z, dev_c, 2)
+    exchange(buf_c, z, dev_c, 2, range(1, 8))
     whole = jnp.sum(buf_c[...], axis=0)
 
     both = jnp.concatenate([whole[:16, :COUNT], whole[:16, COUNT:]], axis=0)
@@ -235,7 +239,7 @@
     vmem = pl.BlockSpec(memory_space=pltpu.VMEM)
     args = (hidden[0], configs, embed, w_up, readout.reshape(1, 512), energies.reshape(1, 1))
     held = [pltpu.VMEM(a.shape, a.dtype) for a in args]
-    sums = pltpu.VMEM((8, 24, 128), jnp.float32)
+    sums = pltpu.VMEM((8, 18, 128), jnp.float32)
     return pl.pallas_call(
         kernel,
         out_shape=jax.ShapeDtypeStruct((ROWS, 512), jnp.float32),

time: 69.6 us -> 65 us (0.934); the launches traced: 68.5 us -> 64.8 us
  Pallas kernels: 66.5 us -> 62.8 us
    pallas_call x1, Pallas kernels: 66.5 us -> 62.8 us  [shards(): pl.pallas_call(kernel, out_shape=jax.ShapeDtypeStruct((ROWS, 512), jnp.fl...]
where the time goes in v3:
time: 65 us; the launch traced here: 64.8 us
  Pallas kernels  62.8 us (97%)
  local copies, waits for them, and re-layouts  1.38 us (2%)
  between operations  0.66 us (1%)
    pallas_call x1, Pallas kernels, shards(): pl.pallas_call(kernel, out_shape=jax.ShapeDtypeStruct((ROWS, 512), jnp.fl...  62.8 us
    unnamed x1, local copies, waits for them, and re-layouts  1.38 us

profile of v3, /device:TPU:1, one launch (start us, length us, event | category | flops | bytes accessed | tf_op | source)
XLA Modules:
  0.0 64.8 jit_solution(784798799960739566)
XLA Ops:
  0.7 62.8 %step.1 = f32[16,512]{1,0:T(8,128)} custom-call(bf16[256,1024]{1,0:T(8,128)(2,1)} %bitcast.4, s32[1,256]{1,0:T(1,128)} %configs_in.1, bf16[4,1024]{1,0:T(4,128)(2,1)} %embed_in.1, bf16[1024,512]{1,0:T(8,128)(2,1)} %w_in.1, f32[1,512]{1,0:T(1,128)} %bitcast.5, f32[1,1]{1,0:T(1,128)} %bitcast.3.energy_in), custom_call_target="tpu_custom_call" | custom-call | tf_op jit(solution)/shard_map/step/pallas_call | solution.py:243
  63.4 1.4 %copy.9 = f32[16,512]{1,0:T(8,128)} copy(f32[16,512]{1,0:T(8,128)} %step.1) | data formatting | bytes 65536

commit v4 on v3

--- a/solution.py
+++ b/solution.py
@@ -14,6 +14,7 @@
 ROWS = 16
 HALF = 32
 PANEL = 8
+CUTS = (0, 384, 512)
 FAR = (4, 3, 5, 2, 6, 1, 7)
 NT = (((1,), (1,)), ((), ()))
 
@@ -36,9 +37,10 @@
 def kernel(
     hidden_in, configs_in, embed_in, w_in, readout_in, energy_in, out,
     hidden, configs, embed, w_up, readout, energy,
-    normed_t, jac, recv, cent, flat, buf_a, buf_b, buf_c, scale,
+    normed_t, jac_0, jac_1, recv_0, recv_1, cent, flat_0, flat_1, buf_a, buf_b, buf_c, scale,
     in_sem, send_sem, recv_sem, ar_send, ar_recv,
 ):
+    jac, recv, flat = (jac_0, jac_1), (recv_0, recv_1), (flat_0, flat_1)
     zh, y, x, zl, c = place()
     me = samp_of(zh, y, x)
     mypar = zl * 2 + c
@@ -96,58 +98,68 @@
     preact = jnp.dot(normed, w_up[...], preferred_element_type=jnp.float32)
     signal = (readout[...] * slope_of(preact)).astype(jnp.bfloat16)
 
-    def piece(dz, dq):
+    def piece(h, dz, dq):
         yq = (y // 2 + dq) % 4
         zt = (zh + dz) % 2
         base = pl.multiple_of(samp_of(zt, yq * 2, 0) * ROWS, 128)
-        block = jnp.dot(normed_t[pl.ds(base, 128), :], signal, preferred_element_type=jnp.float32)
-        jac[pl.ds(base, 128), :] = block.astype(jnp.bfloat16)
+        block = jnp.dot(
+            normed_t[pl.ds(base, 128), :], signal[:, CUTS[h]:CUTS[h + 1]],
+            preferred_element_type=jnp.float32)
+        jac[h][pl.ds(base, 128), :] = block.astype(jnp.bfloat16)
         return zt, yq
 
-    def send(zt, yt, k):
+    def send(h, zt, yt, k):
         t = (zt * 8 + yt) * 4 + xs[k]
         pltpu.make_async_remote_copy(
-            src_ref=jac.at[pl.ds(pl.multiple_of(t * ROWS, ROWS), ROWS)],
-            dst_ref=recv.at[me],
-            send_sem=send_sem,
-            recv_sem=recv_sem,
+            src_ref=jac[h].at[pl.ds(pl.multiple_of(t * ROWS, ROWS), ROWS)],
+            dst_ref=recv[h].at[me],
+            send_sem=send_sem.at[h],
+            recv_sem=recv_sem.at[h],
             device_id=(t, mypar),
             device_id_type=MESH,
         ).start()
 
     sides = (y % 2, (y + 1) % 2)
-    for n, (dz, dq) in enumerate(((1, 2), (0, 2), (1, 1), (0, 1), (1, 3), (0, 3), (1, 0), (0, 0))):
-        zt, yq = piece(dz, dq)
-        if n == 0:
-            pl.semaphore_wait(barrier, 73)
-        for k in range(4):
-            for dr in (1, 0):
-                if (dz, dq, k, dr) != (0, 0, 3, 0):
-                    send(zt, yq * 2 + sides[dr], k)
-    recv[me] = jac[pl.ds(pl.multiple_of(me * ROWS, ROWS), ROWS), :]
-
-    pltpu.make_async_copy(recv.at[pl.ds(0, 63)], recv.at[pl.ds(0, 63)], recv_sem).wait()
-
-    def add(s, total):
-        return total + recv[s].astype(jnp.float32)
-
-    total = lax.fori_loop(0, COUNT, add, jnp.zeros((ROWS, 512), jnp.float32), unroll=8)
-    mean = total * (1.0 / COUNT)
-
-    def center(s, carry):
-        v = ((recv[s].astype(jnp.float32) - mean) * 0.125).astype(jnp.bfloat16)
-        for j in range(4):
-            cent[j, pl.ds(pl.multiple_of(s * ROWS, ROWS), ROWS), :] = (
-                v[:, j * 128:(j + 1) * 128].astype(jnp.float32))
-        return carry
-
-    lax.fori_loop(0, COUNT, center, 0, unroll=8)
-
-    for i in range(ROWS):
-        for j in range(4):
-            at = (i * 4 + j) * 128
-            flat[:, at:at + 128] = cent[j, pl.ds(i, COUNT, stride=ROWS), :].astype(jnp.bfloat16)
-    gram = lax.dot_general(flat[...], flat[...], NT, preferred_element_type=jnp.float32)
+    steps = ((1, 2), (0, 1), (1, 3), (0, 2), (1, 1), (0, 3), (1, 0), (0, 0))
+    for h in range(2):
+        for n, (dz, dq) in enumerate(steps):
+            zt, yq = piece(h, dz, dq)
+            if h == 0 and n == 0:
+                pl.semaphore_wait(barrier, 73)
+            for k in range(4):
+                for dr in (1, 0):
+                    if (dz, dq, k, dr) != (0, 0, 3, 0):
+                        send(h, zt, yq * 2 + sides[dr], k)
+        recv[h][me] = jac[h][pl.ds(pl.multiple_of(me * ROWS, ROWS), ROWS), :]
+
+    gram = jnp.zeros((COUNT, COUNT), jnp.float32)
+    for h in range(2):
+        first, blocks = CUTS[h] // 128, (CUTS[h + 1] - CUTS[h]) // 128
+        got = recv[h].at[pl.ds(0, 63)]
+        pltpu.make_async_copy(got, got, recv_sem.at[h]).wait()
+
+        def add(s, total):
+            return total + recv[h][s].astype(jnp.float32)
+
+        total = lax.fori_loop(0, COUNT, add, jnp.zeros((ROWS, CUTS[h + 1] - CUTS[h]), jnp.float32), unroll=8)
+        mean = total * (1.0 / COUNT)
+
+        def center(s, carry):
+            v = ((recv[h][s].astype(jnp.float32) - mean) * 0.125).astype(jnp.bfloat16)
+            for j in range(blocks):
+                cent[first + j, pl.ds(pl.multiple_of(s * ROWS, ROWS), ROWS), :] = (
+                    v[:, j * 128:(j + 1) * 128].astype(jnp.float32))
+            return carry
+
+        lax.fori_loop(0, COUNT, center, 0, unroll=8)
+
+        for i in range(ROWS):
+            for j in range(blocks):
+                at = (i * blocks + j) * 128
+                flat[h][:, at:at + 128] = (
+                    cent[first + j, pl.ds(i, COUNT, stride=ROWS), :].astype(jnp.bfloat16))
+        gram += lax.dot_general(flat[h][...], flat[h][...], NT, preferred_element_type=jnp.float32)
+
     up, left, low = gram[:HALF, :HALF], gram[HALF:, :HALF], gram[HALF:, HALF:]
     r32 = lax.broadcasted_iota(jnp.int32, (HALF, HALF), 0)
     c32 = lax.broadcasted_iota(jnp.int32, (HALF, HALF), 1)
@@ -229,7 +241,9 @@
     for j in range(4):
         out[:, j * 128:(j + 1) * 128] = -trace_mean * applied[j]
 
-    pltpu.make_async_copy(recv.at[pl.ds(0, 63)], recv.at[pl.ds(0, 63)], send_sem).wait()
+    for h in range(2):
+        sent = recv[h].at[pl.ds(0, 63)]
+        pltpu.make_async_copy(sent, sent, send_sem.at[h]).wait()
     for own, buf in enumerate((buf_a, buf_b, buf_c)):
         settle_send(buf, own)
 
@@ -239,6 +253,7 @@
     vmem = pl.BlockSpec(memory_space=pltpu.VMEM)
     args = (hidden[0], configs, embed, w_up, readout.reshape(1, 512), energies.reshape(1, 1))
     held = [pltpu.VMEM(a.shape, a.dtype) for a in args]
+    widths = (CUTS[1], CUTS[2] - CUTS[1])
     sums = pltpu.VMEM((8, 18, 128), jnp.float32)
     return pl.pallas_call(
         kernel,
@@ -247,15 +262,15 @@
         out_specs=vmem,
         scratch_shapes=held + [
             pltpu.VMEM((1024, 256), jnp.bfloat16),
-            pltpu.VMEM((1024, 512), jnp.bfloat16),
-            pltpu.VMEM((COUNT, ROWS, 512), jnp.bfloat16),
+            *[pltpu.VMEM((1024, w), jnp.bfloat16) for w in widths],
+            *[pltpu.VMEM((COUNT, ROWS, w), jnp.bfloat16) for w in widths],
             pltpu.VMEM((4, COUNT * ROWS, 128), jnp.float32),
-            pltpu.VMEM((COUNT, 8192), jnp.bfloat16),
+            *[pltpu.VMEM((COUNT, ROWS * w), jnp.bfloat16) for w in widths],
             sums, sums, sums,
             pltpu.VMEM((COUNT, 128), jnp.float32),
             pltpu.SemaphoreType.DMA((6,)),
-            pltpu.SemaphoreType.DMA,
-            pltpu.SemaphoreType.DMA,
+            pltpu.SemaphoreType.DMA((2,)),
+            pltpu.SemaphoreType.DMA((2,)),
             pltpu.SemaphoreType.DMA((3,)),
             pltpu.SemaphoreType.DMA((3,)),
         ],

time: 65 us -> 63.6 us (0.978)
  Pallas kernels: 62.8 us -> 61.3 us
    pallas_call x1, Pallas kernels: 62.8 us -> 61.3 us  [shards(): pl.pallas_call(kernel, out_shape=jax.ShapeDtypeStruct((ROWS, 512), jnp.fl...]
where the time goes in v4:
time: 63.6 us; the launch traced here: 63.4 us
  Pallas kernels  61.3 us (96%)
  local copies, waits for them, and re-layouts  1.38 us (2%)
  between operations  0.66 us (1%)
    pallas_call x1, Pallas kernels, shards(): pl.pallas_call(kernel, out_shape=jax.ShapeDtypeStruct((ROWS, 512), jnp.fl...  61.3 us
    unnamed x1, local copies, waits for them, and re-layouts  1.38 us

profile of v4, /device:TPU:1, one launch (start us, length us, event | category | flops | bytes accessed | tf_op | source)
XLA Modules:
  0.0 63.4 jit_solution(3614145016697724796)
XLA Ops:
  0.7 61.3 %step.1 = f32[16,512]{1,0:T(8,128)} custom-call(bf16[256,1024]{1,0:T(8,128)(2,1)} %bitcast.4, s32[1,256]{1,0:T(1,128)} %configs_in.1, bf16[4,1024]{1,0:T(4,128)(2,1)} %embed_in.1, bf16[1024,512]{1,0:T(8,128)(2,1)} %w_in.1, f32[1,512]{1,0:T(1,128)} %bitcast.5, f32[1,1]{1,0:T(1,128)} %bitcast.3.energy_in), custom_call_target="tpu_custom_call" | custom-call | tf_op jit(solution)/shard_map/step/pallas_call | solution.py:258
  62.0 1.4 %copy.9 = f32[16,512]{1,0:T(8,128)} copy(f32[16,512]{1,0:T(8,128)} %step.1) | data formatting | bytes 65536

commit v5 on v4

--- a/solution.py
+++ b/solution.py
@@ -48,14 +48,6 @@
     slot_a = x * 2 + c
 
     barrier = pltpu.get_barrier_semaphore()
-
-    for dz in FAR:
-        zt = (z + dz) % 8
-        if dz == 4:
-            continue
-        pl.semaphore_signal(
-            barrier, inc=1,
-            device_id=(samp_of(zt // 4, y, x), (zt % 4) * 2 + c), device_id_type=MESH)
 
     ys = [(y + dy) % 8 for dy in FAR + (0,)]
     xs = [(x + dx) % 4 for dx in (2, 1, 3, 0)]
@@ -72,6 +64,14 @@
             barrier, inc=1,
             device_id=(samp_of(zh, y, (x + dx) % 4), zl * 2 + (1 - c)), device_id_type=MESH)
 
+    for dz in FAR:
+        zt = (z + dz) % 8
+        if dz == 4:
+            continue
+        pl.semaphore_signal(
+            barrier, inc=1,
+            device_id=(samp_of(zt // 4, y, x), (zt % 4) * 2 + c), device_id_type=MESH)
+
     loads = [
         pltpu.make_async_copy(src, dst, in_sem.at[n])
         for n, (src, dst) in enumerate((
@@ -95,15 +95,18 @@
     normed_t[...] = normed.T
     for load in loads[3:]:
         load.wait()
-    preact = jnp.dot(normed, w_up[...], preferred_element_type=jnp.float32)
-    signal = (readout[...] * slope_of(preact)).astype(jnp.bfloat16)
-
-    def piece(h, dz, dq):
+
+    def signal_of(h):
+        span = slice(CUTS[h], CUTS[h + 1])
+        preact = jnp.dot(normed, w_up[:, span], preferred_element_type=jnp.float32)
+        return (readout[:, span] * slope_of(preact)).astype(jnp.bfloat16)
+
+    def piece(h, signal, dz, dq):
         yq = (y // 2 + dq) % 4
         zt = (zh + dz) % 2
         base = pl.multiple_of(samp_of(zt, yq * 2, 0) * ROWS, 128)
         block = jnp.dot(
-            normed_t[pl.ds(base, 128), :], signal[:, CUTS[h]:CUTS[h + 1]],
+            normed_t[pl.ds(base, 128), :], signal,
             preferred_element_type=jnp.float32)
         jac[h][pl.ds(base, 128), :] = block.astype(jnp.bfloat16)
         return zt, yq
@@ -122,8 +125,9 @@
     sides = (y % 2, (y + 1) % 2)
     steps = ((1, 2), (0, 1), (1, 3), (0, 2), (1, 1), (0, 3), (1, 0), (0, 0))
     for h in range(2):
+        signal = signal_of(h)
         for n, (dz, dq) in enumerate(steps):
-            zt, yq = piece(h, dz, dq)
+            zt, yq = piece(h, signal, dz, dq)
             if h == 0 and n == 0:
                 pl.semaphore_wait(barrier, 73)
             for k in range(4):
@@ -141,7 +145,7 @@
         def add(s, total):
             return total + recv[h][s].astype(jnp.float32)
 
-        total = lax.fori_loop(0, COUNT, add, jnp.zeros((ROWS, CUTS[h + 1] - CUTS[h]), jnp.float32), unroll=8)
+        total = lax.fori_loop(0, COUNT, add, jnp.zeros((ROWS, CUTS[h + 1] - CUTS[h]), jnp.float32), unroll=16)
         mean = total * (1.0 / COUNT)
 
         def center(s, carry):
@@ -151,7 +155,7 @@
                     v[:, j * 128:(j + 1) * 128].astype(jnp.float32))
             return carry
 
-        lax.fori_loop(0, COUNT, center, 0, unroll=8)
+        lax.fori_loop(0, COUNT, center, 0, unroll=16)
 
         for i in range(ROWS):
             for j in range(blocks):
@@ -237,7 +241,7 @@
         return tuple(a + w * cent[j, at, :] for j, a in enumerate(acc))
 
     zero = jnp.zeros((ROWS, 128), jnp.float32)
-    applied = lax.fori_loop(0, COUNT, apply, (zero,) * 4, unroll=8)
+    applied = lax.fori_loop(0, COUNT, apply, (zero,) * 4, unroll=16)
     for j in range(4):
         out[:, j * 128:(j + 1) * 128] = -trace_mean * applied[j]
 

time: 63.6 us -> 63.5 us (level)
  no operation moved by 1% of the time
where the time goes in v5:
time: 63.5 us; the launch traced here: 63.2 us
  Pallas kernels  61.1 us (96%)
  local copies, waits for them, and re-layouts  1.38 us (2%)
  between operations  0.66 us (1%)
    pallas_call x1, Pallas kernels, shards(): pl.pallas_call(kernel, out_shape=jax.ShapeDtypeStruct((ROWS, 512), jnp.fl...  61.1 us
    unnamed x1, local copies, waits for them, and re-layouts  1.38 us

profile of v5, /device:TPU:1, one launch (start us, length us, event | category | flops | bytes accessed | tf_op | source)
XLA Modules:
  0.0 63.2 jit_solution(12015824777074355351)
XLA Ops:
  0.7 61.1 %step.1 = f32[16,512]{1,0:T(8,128)} custom-call(bf16[256,1024]{1,0:T(8,128)(2,1)} %bitcast.4, s32[1,256]{1,0:T(1,128)} %configs_in.1, bf16[4,1024]{1,0:T(4,128)(2,1)} %embed_in.1, bf16[1024,512]{1,0:T(8,128)(2,1)} %w_in.1, f32[1,512]{1,0:T(1,128)} %bitcast.5, f32[1,1]{1,0:T(1,128)} %bitcast.3.energy_in), custom_call_target="tpu_custom_call" | custom-call | tf_op jit(solution)/shard_map/step/pallas_call | solution.py:262
  61.8 1.4 %copy.9 = f32[16,512]{1,0:T(8,128)} copy(f32[16,512]{1,0:T(8,128)} %step.1) | data formatting | bytes 65536

commit v6 on v4

--- a/solution.py
+++ b/solution.py
@@ -37,7 +37,7 @@
 def kernel(
     hidden_in, configs_in, embed_in, w_in, readout_in, energy_in, out,
     hidden, configs, embed, w_up, readout, energy,
-    normed_t, jac_0, jac_1, recv_0, recv_1, cent, flat_0, flat_1, buf_a, buf_b, buf_c, scale,
+    normed_t, jac_0, jac_1, recv_0, recv_1, cent, flat_0, flat_1, buf_k, buf_a, buf_b, buf_c, scale,
     in_sem, send_sem, recv_sem, ar_send, ar_recv,
 ):
     jac, recv, flat = (jac_0, jac_1), (recv_0, recv_1), (flat_0, flat_1)
@@ -45,7 +45,6 @@
     me = samp_of(zh, y, x)
     mypar = zl * 2 + c
     z = zh * 4 + zl
-    slot_a = x * 2 + c
 
     barrier = pltpu.get_barrier_semaphore()
 
@@ -67,10 +66,8 @@
                     continue
                 pl.semaphore_signal(
                     barrier, inc=1, device_id=(line + xt, mypar), device_id_type=MESH)
-    for dx in (2, 1, 3, 0):
-        pl.semaphore_signal(
-            barrier, inc=1,
-            device_id=(samp_of(zh, y, (x + dx) % 4), zl * 2 + (1 - c)), device_id_type=MESH)
+    pl.semaphore_signal(
+        barrier, inc=1, device_id=(me, zl * 2 + 1 - c), device_id_type=MESH)
 
     loads = [
         pltpu.make_async_copy(src, dst, in_sem.at[n])
@@ -125,7 +122,7 @@
         for n, (dz, dq) in enumerate(steps):
             zt, yq = piece(h, dz, dq)
             if h == 0 and n == 0:
-                pl.semaphore_wait(barrier, 73)
+                pl.semaphore_wait(barrier, 70)
             for k in range(4):
                 for dr in (1, 0):
                     if (dz, dq, k, dr) != (0, 0, 3, 0):
@@ -169,8 +166,8 @@
     tail_row = lax.broadcasted_iota(jnp.int32, (8, 128), 0)
     tail_lane = lax.broadcasted_iota(jnp.int32, (8, 128), 1)
     mine = jnp.where((tail_row == 1) & (tail_lane == me), energy[...] * 0.125, 0.0)
-    buf_a[slot_a, 0:16] = jnp.concatenate([both[:16], both[16:]], axis=1)
-    buf_a[slot_a, 16:18] = jnp.where(tail_row == 0, low_diag, mine)[:2]
+    buf_k[c, 0:16] = jnp.concatenate([both[:16], both[16:]], axis=1)
+    buf_k[c, 16:18] = jnp.where(tail_row == 0, low_diag, mine)[:2]
 
     def exchange(buf, slot, target_of, own, steps):
         for d in steps:
@@ -178,13 +175,18 @@
                 src_ref=buf.at[slot], dst_ref=buf.at[slot],
                 send_sem=ar_send.at[own], recv_sem=ar_recv.at[own],
                 device_id=target_of(d), device_id_type=MESH).start()
-        pltpu.make_async_copy(buf.at[pl.ds(0, 7)], buf.at[pl.ds(0, 7)], ar_recv.at[own]).wait()
+        some = buf.at[pl.ds(0, buf.shape[0] - 1)]
+        pltpu.make_async_copy(some, some, ar_recv.at[own]).wait()
 
     def settle_send(buf, own):
-        pltpu.make_async_copy(buf.at[pl.ds(0, 7)], buf.at[pl.ds(0, 7)], ar_send.at[own]).wait()
+        some = buf.at[pl.ds(0, buf.shape[0] - 1)]
+        pltpu.make_async_copy(some, some, ar_send.at[own]).wait()
+
+    def dev_k(d):
+        return (me, zl * 2 + 1 - c)
 
     def dev_a(d):
-        return (samp_of(zh, y, (x + d // 2) % 4), zl * 2 + (c + d) % 2)
+        return (samp_of(zh, y, (x + d) % 4), mypar)
 
     def dev_b(d):
         return (samp_of(zh, (y + d) % 8, x), mypar)
@@ -193,7 +195,9 @@
         zt = (z + d) % 8
         return (samp_of(zt // 4, y, x), (zt % 4) * 2 + c)
 
-    exchange(buf_a, slot_a, dev_a, 0, (1, 2, 3, 4, 5, 6, 7))
+    exchange(buf_k, c, dev_k, 3, (1,))
+    buf_a[x] = jnp.sum(buf_k[...], axis=0)
+    exchange(buf_a, x, dev_a, 0, (2, 1, 3))
     buf_b[y] = jnp.sum(buf_a[...], axis=0)
     exchange(buf_b, y, dev_b, 1, range(1, 8))
     buf_c[z] = jnp.sum(buf_b[...], axis=0)
@@ -244,7 +248,7 @@
     for h in range(2):
         sent = recv[h].at[pl.ds(0, 63)]
         pltpu.make_async_copy(sent, sent, send_sem.at[h]).wait()
-    for own, buf in enumerate((buf_a, buf_b, buf_c)):
+    for own, buf in enumerate((buf_a, buf_b, buf_c, buf_k)):
         settle_send(buf, own)
 
 
@@ -266,13 +270,15 @@
             *[pltpu.VMEM((COUNT, ROWS, w), jnp.bfloat16) for w in widths],
             pltpu.VMEM((4, COUNT * ROWS, 128), jnp.float32),
             *[pltpu.VMEM((COUNT, ROWS * w), jnp.bfloat16) for w in widths],
-            sums, sums, sums,
+            pltpu.VMEM((2, 18, 128), jnp.float32),
+            pltpu.VMEM((4, 18, 128), jnp.float32),
+            sums, sums,
             pltpu.VMEM((COUNT, 128), jnp.float32),
             pltpu.SemaphoreType.DMA((6,)),
             pltpu.SemaphoreType.DMA((2,)),
             pltpu.SemaphoreType.DMA((2,)),
-            pltpu.SemaphoreType.DMA((3,)),
-            pltpu.SemaphoreType.DMA((3,)),
+            pltpu.SemaphoreType.DMA((4,)),
+            pltpu.SemaphoreType.DMA((4,)),
         ],
         compiler_params=pltpu.CompilerParams(
             collective_id=0, has_side_effects=True, vmem_limit_bytes=56 << 20),

time: 63.6 us -> 64 us (level)
  no operation moved by 1% of the time
where the time goes in v6:
time: 64 us; the launch traced here: 63.8 us
  Pallas kernels  61.7 us (96%)
  local copies, waits for them, and re-layouts  1.38 us (2%)
  between operations  0.66 us (1%)
    pallas_call x1, Pallas kernels, shards(): pl.pallas_call(kernel, out_shape=jax.ShapeDtypeStruct((ROWS, 512), jnp.fl...  61.7 us
    unnamed x1, local copies, waits for them, and re-layouts  1.38 us

profile of v6, /device:TPU:1, one launch (start us, length us, event | category | flops | bytes accessed | tf_op | source)
XLA Modules:
  0.0 63.8 jit_solution(15487935793579176233)
XLA Ops:
  0.7 61.7 %step.1 = f32[16,512]{1,0:T(8,128)} custom-call(bf16[256,1024]{1,0:T(8,128)(2,1)} %bitcast.4, s32[1,256]{1,0:T(1,128)} %configs_in.1, bf16[4,1024]{1,0:T(4,128)(2,1)} %embed_in.1, bf16[1024,512]{1,0:T(8,128)(2,1)} %w_in.1, f32[1,512]{1,0:T(1,128)} %bitcast.5, f32[1,1]{1,0:T(1,128)} %bitcast.3.energy_in), custom_call_target="tpu_custom_call" | custom-call | tf_op jit(solution)/shard_map/step/pallas_call | solution.py:262
  62.4 1.4 %copy.9 = f32[16,512]{1,0:T(8,128)} copy(f32[16,512]{1,0:T(8,128)} %step.1) | data formatting | bytes 65536
